TPU v7x, 256 devices: a whole 4x4x8 slice. The times are simulated.
256 devices in a mesh: row: 4 (over x), col: 4 (over y), depth: 16 (over z, core).
Axes of the slice: x: 4, y: 4, z: 8, core: 2. Of those that a mesh axis runs over, the one named last changes fastest.
Arguments:
- pair: bfloat16 [640, 640, 128], P('row', 'col'), may hold values from -6 to 6
- in_gain: float32 [2, 128], replicated, may hold values from 0.25 to 1.75
- in_bias: float32 [2, 128], replicated, may hold values from -3 to 3
- proj_weight: bfloat16 [2, 128, 512], replicated, may hold values from -0.5 to 0.5
- gate_weight: bfloat16 [2, 128, 128], replicated, may hold values from -0.5 to 0.5
- out_gain: float32 [2, 128], replicated, may hold values from 0.25 to 1.75
- out_bias: float32 [2, 128], replicated, may hold values from -3 to 3
- out_weight: bfloat16 [2, 128, 128], replicated, may hold values from -0.5 to 0.5
Outputs:
- updated: bfloat16 [640, 640, 128], P('row', 'col')
All inputs are finite; a program needn't handle non-finite values.
Results may differ from a plain program's by a relative error of at most 0.015.
Values may be sent and summed in bfloat16 or wider, within the bound.
No kernel may reach another device: no remote copies, remote signals or barrier semaphores. Data moves between devices by JAX's collectives and lax.ppermute only.
A program may use at most 128 MiB of HBM per device.

v0:
```python
import jax
import jax.numpy as jnp
from jax import lax
from jax.sharding import PartitionSpec as P


def normalize(values, gain, bias):
    values = values.astype(jnp.float32)
    mean = jnp.mean(values, axis=-1, keepdims=True)
    centred = values - mean
    spread = jnp.mean(centred * centred, axis=-1, keepdims=True)
    return centred * lax.rsqrt(spread + 1e-05) * gain + bias


def gated(normed, weight):
    width = weight.shape[1] // 2
    hidden = jnp.dot(normed, weight, preferred_element_type=jnp.float32)
    return (jax.nn.sigmoid(hidden[..., width:]) * hidden[..., :width]).astype(jnp.bfloat16)


def pick_rows(values, group, part, layer):
    length = values.shape[0]
    shaped = values.reshape((length // group, group) + values.shape[1:])
    taken = lax.dynamic_slice_in_dim(shaped, layer * part, part, 1)
    return taken.reshape((length // group * part,) + values.shape[1:])


def pick_cols(values, group, part, layer):
    rows_here, length, chans = values.shape
    shaped = values.reshape(rows_here, length // group, group, chans)
    taken = lax.dynamic_slice_in_dim(shaped, layer * part, part, 2)
    return taken.reshape(rows_here, length // group * part, chans)


def order_rows(gathered, depth, part):
    total, cols_here, chans = gathered.shape
    shaped = gathered.reshape(depth, total // (depth * part), part, cols_here, chans)
    return jnp.transpose(shaped, (1, 0, 2, 3, 4)).reshape(total, cols_here, chans)


def order_cols(gathered, depth, part):
    rows_here, total, chans = gathered.shape
    shaped = gathered.reshape(rows_here, depth, total // (depth * part), part, chans)
    return jnp.transpose(shaped, (0, 2, 1, 3, 4)).reshape(rows_here, total, chans)


def finish(field_part, normed_part, tri, gate_w, gain, bias, weight):
    gate = jax.nn.sigmoid(jnp.dot(normed_part, gate_w, preferred_element_type=jnp.float32))
    upd = normalize(tri, gain, bias).astype(jnp.bfloat16)
    result = field_part.astype(jnp.float32) + gate * jnp.dot(
        upd, weight, preferred_element_type=jnp.float32
    )
    return result.astype(jnp.bfloat16)


def on_device(pair, in_gain, in_bias, proj_weight, gate_weight, out_gain, out_bias, out_weight):
    rows_tile, cols_tile, chans = pair.shape
    depth = lax.axis_size("depth")
    layer = lax.axis_index("depth")
    group = min(rows_tile, cols_tile)
    part = group // depth
    first_w = proj_weight[0]
    second_w = proj_weight[1]
    normed = normalize(pair, in_gain[0], in_bias[0]).astype(jnp.bfloat16)
    block = rows_tile // depth
    own_rows = lax.dynamic_slice_in_dim(normed, layer * block, block, 0)
    left = lax.all_gather(gated(own_rows, first_w[:, : 2 * chans]), "depth", axis=0, tiled=True)
    right = gated(pick_rows(normed, group, part, layer), first_w[:, 2 * chans :])
    partial_value = jnp.einsum(
        "jkc,ikc->jic",
        lax.all_gather(right, "row", axis=0, tiled=True),
        left,
        preferred_element_type=jnp.float32,
    )
    summed = lax.psum_scatter(
        partial_value.astype(jnp.bfloat16), "col", scatter_dimension=0, tiled=True
    ).astype(jnp.float32)
    tri = jnp.transpose(summed, (1, 0, 2))
    pair_cols = pick_cols(pair, group, part, layer)
    normed_cols = pick_cols(normed, group, part, layer)
    middle = finish(
        pair_cols, normed_cols, tri, gate_weight[0], out_gain[0], out_bias[0], out_weight[0]
    )
    normed_share = normalize(middle, in_gain[1], in_bias[1]).astype(jnp.bfloat16)
    right_share = gated(normed_share, second_w[:, 2 * chans :])
    whole_g, right_g = (
        lax.all_gather(middle, "depth", axis=1, tiled=True),
        lax.all_gather(right_share, "depth", axis=1, tiled=True),
    )
    whole = order_cols(whole_g, depth, part)
    right_in = order_cols(right_g, depth, part)
    left_in = gated(normed_share, second_w[:, : 2 * chans])
    partial_in = jnp.einsum(
        "kic,kjc->ijc",
        lax.all_gather(left_in, "col", axis=1, tiled=True),
        right_in,
        preferred_element_type=jnp.float32,
    )
    tri_in = lax.psum_scatter(
        partial_in.astype(jnp.bfloat16), "row", scatter_dimension=0, tiled=True
    ).astype(jnp.float32)
    middle_rows = pick_rows(whole, group, part, layer)
    normed_rows = normalize(middle_rows, in_gain[1], in_bias[1]).astype(jnp.bfloat16)
    result = finish(
        middle_rows, normed_rows, tri_in, gate_weight[1], out_gain[1], out_bias[1], out_weight[1]
    )
    gathered = lax.all_gather(result, "depth", axis=0, tiled=True)
    return order_rows(gathered, depth, part)


def solution(mesh):
    placed = (P("row", "col", None), P(), P(), P(), P(), P(), P(), P())
    return jax.shard_map(
        on_device, mesh=mesh, in_specs=placed, out_specs=P("row", "col", None), check_vma=False
    )
```

profile of v0, /device:TPU:1, one launch (start us, length us, event | category | flops | bytes accessed | tf_op | source)
XLA Modules:
  0.0 409.9 jit_solution(17260253756883314831)
XLA Ops:
  6.5 8.5 %convert_reduce_fusion = f32[160,160]{0,1:T(8,128)S(1)} fusion(bf16[160,160,128]{2,1,0:T(8,128)(2,1)} %param.8), kind=kLoop, calls=%fused_computation.1 | loop fusion | flops 6528000 | bytes 6656000 | tf_op jit(solution)/shard_map/reduce_sum | solution.py:9
  15.1 12.3 %fusion.2 = f32[160,160]{0,1:T(8,128)S(1)} fusion(f32[160,160]{0,1:T(8,128)S(1)} %broadcast_multiply_fusion, bf16[160,160,128]{2,1,0:T(8,128)(2,1)S(1)} %copy-done), kind=kLoop, calls=%fused_computation.4 | loop fusion | flops 13081600 | bytes 6758400 | tf_op jit(solution)/shard_map/reduce_sum | solution.py:11
  27.5 9.5 %fusion.5 = bf16[160,160,128]{2,0,1:T(8,128)(2,1)S(1)} fusion(f32[128]{0:T(128)S(1)} %get-tuple-element.13, f32[128]{0:T(128)S(1)} %get-tuple-element.18, f32[160,160]{0,1:T(8,128)S(1)} %add_rsqrt_fusion, f32[160,160]{0,1:T(8,128)S(1)} %broadcast_multiply_fusion, bf16[160,160,128]{2,1,0:T(8,128)(2,1)} %param.8), kind=kLoop, calls=%fused_computation.7 | loop fusion | flops 19660800 | bytes 13313024 | tf_op jit(solution)/shard_map/convert_element_type | solution.py:64
  37.0 2.8 copy-done.2
  41.9 1.0 fusion.46
  42.9 32.1 %all-gather.9.cloned.1.call-done = bf16[40,160,128]{2,1,0:T(8,128)(2,1)} async-done(((bf16[10,160,128]{2,1,0:T(8,128)(2,1)}), bf16[40,160,128]{2,1,0:T(8,128)(2,1)}) %all-gather.9.cloned.1.call-update) | async-done | bytes 1638416 | tf_op jit(solution)/shard_map/all_gather | solution.py:71
  75.0 3.7 copy.34
  78.7 45.9 %all-gather.7.cloned.1.call-done = bf16[160,160,128]{2,1,0:T(8,128)(2,1)} async-done(((bf16[10,160,128]{2,1,0:T(8,128)(2,1)}), bf16[160,160,128]{2,1,0:T(8,128)(2,1)}) %all-gather.7.cloned.1.call-update) | async-done | bytes 6553616 | tf_op jit(solution)/shard_map/all_gather | solution.py:67
  124.5 15.1 %copy.33 = bf16[160,160,128]{1,0,2:T(8,128)(2,1)} copy(bf16[160,160,128]{2,1,0:T(8,128)(2,1)} %all-gather.7.cloned.1.call-done) | data formatting | bytes 13107200 | tf_op jit(solution)/shard_map/all_gather | solution.py:67
  139.6 8.8 %convert_bitcast_fusion.1 = bf16[40,160,128]{1,0,2:T(8,128)(2,1)} fusion(bf16[160,160,128]{1,0,2:T(8,128)(2,1)} %copy.33, bf16[40,160,128]{1,0,2:T(8,128)(2,1)S(1)} %copy.34), kind=kOutput, calls=%fused_computation.9 | convolution fusion | flops 262963200 | bytes 9830400 | tf_op jit(solution)/shard_map/jkc,ikc->jic/dot_general | solution.py:69
  148.4 4.6 %copy.35 = bf16[40,160,128]{2,1,0:T(8,128)(2,1)} copy(bf16[40,160,128]{1,0,2:T(8,128)(2,1)} %convert_bitcast_fusion.1) | data formatting | bytes 3276800 | tf_op jit(solution)/shard_map/convert_element_type | solution.py:76
  153.3 8.1 %copy.29 = bf16[160,160,128]{2,0,1:T(8,128)(2,1)} copy(bf16[160,160,128]{2,1,0:T(8,128)(2,1)} %param.8) | data formatting | bytes 13107200 | tf_op args[0]
  161.4 1.4 fusion.13
  162.8 16.7 %reduce-scatter.3.cloned.1.call-done = bf16[10,160,128]{2,1,0:T(8,128)(2,1)} async-done(((bf16[40,160,128]{2,1,0:T(8,128)(2,1)}), bf16[10,160,128]{2,1,0:T(8,128)(2,1)}) %reduce-scatter.3.cloned.1.call-update) | async-done | bytes 409616 | tf_op jit(solution)/shard_map/reduce_scatter | solution.py:75
  179.5 1.2 bitcast_reduce_fusion
  180.8 1.7 fusion.52
  182.5 2.0 convert_reduce_fusion.3
  185.8 1.0 fusion.34
  189.1 27.6 %all-gather.15.cloned.1.call-done = bf16[160,40,128]{2,0,1:T(8,128)(2,1)} async-done(((bf16[160,10,128]{2,0,1:T(8,128)(2,1)}), bf16[160,40,128]{2,0,1:T(8,128)(2,1)}) %all-gather.15.cloned.1.call-update) | async-done | bytes 1638416 | tf_op jit(solution)/shard_map/all_gather | solution.py:95
  216.7 3.7 copy.38
  220.4 45.8 %all-gather.13.cloned.1.call-done = bf16[160,160,128]{2,0,1:T(8,128)(2,1)} async-done(((bf16[160,10,128]{2,0,1:T(8,128)(2,1)}), bf16[160,160,128]{2,0,1:T(8,128)(2,1)}) %all-gather.13.cloned.1.call-update) | async-done | bytes 6553616 | tf_op jit(solution)/shard_map/all_gather | solution.py:88
  266.2 15.1 %copy.37 = bf16[160,160,128]{0,1,2:T(8,128)(2,1)} copy(bf16[160,160,128]{2,0,1:T(8,128)(2,1)} %all-gather.13.cloned.1.call-done) | data formatting | bytes 13107200 | tf_op jit(solution)/shard_map/all_gather | solution.py:88
  281.3 8.9 %convert_bitcast_fusion = bf16[40,160,128]{1,0,2:T(8,128)(2,1)} fusion(bf16[160,160,128]{0,1,2:T(8,128)(2,1)} %copy.37, bf16[160,40,128]{0,1,2:T(8,128)(2,1)S(1)} %copy.38), kind=kOutput, calls=%fused_computation.8 | convolution fusion | flops 262963200 | bytes 9830400 | tf_op jit(solution)/shard_map/kic,kjc->ijc/dot_general | solution.py:93
  290.1 4.7 %copy.39 = bf16[40,160,128]{2,1,0:T(8,128)(2,1)} copy(bf16[40,160,128]{1,0,2:T(8,128)(2,1)} %convert_bitcast_fusion) | data formatting | bytes 3276800 | tf_op jit(solution)/shard_map/convert_element_type | solution.py:100
  295.1 18.8 %all-gather.11.cloned.1.call-done = bf16[160,160,128]{2,0,1:T(8,128)(2,1)} async-done(((bf16[160,10,128]{2,0,1:T(8,128)(2,1)}), bf16[160,160,128]{2,0,1:T(8,128)(2,1)}) %all-gather.11.cloned.1.call-update) | async-done | bytes 6553616 | tf_op jit(solution)/shard_map/all_gather | solution.py:87
  313.9 1.5 constant_dynamic-slice_fusion
  317.2 25.9 %reduce-scatter.5.cloned.1.call-done = bf16[10,160,128]{2,1,0:T(8,128)(2,1)} async-done(((bf16[40,160,128]{2,1,0:T(8,128)(2,1)}), bf16[10,160,128]{2,1,0:T(8,128)(2,1)}) %reduce-scatter.5.cloned.1.call-update) | async-done | bytes 409616 | tf_op jit(solution)/shard_map/reduce_scatter | solution.py:99
  343.1 1.2 convert_reduce_fusion.2
  344.3 1.7 fusion.26
  346.0 2.4 fusion.15
  348.4 47.9 %all-gather.17.cloned.1.call-done = bf16[160,160,128]{2,1,0:T(8,128)(2,1)} async-done(((bf16[10,160,128]{2,1,0:T(8,128)(2,1)}), bf16[160,160,128]{2,1,0:T(8,128)(2,1)}) %all-gather.17.cloned.1.call-update) | async-done | bytes 6553616 | tf_op jit(solution)/shard_map/all_gather | solution.py:107
  396.3 6.8 %copy.60 = bf16[160,160,128]{2,1,0:T(8,128)(2,1)} copy(bf16[160,160,128]{2,1,0:T(8,128)(2,1)} %all-gather.17.cloned.1.call-done) | data formatting | bytes 13107200
  (59 shorter events, 8.1 us)
Async XLA Ops:
  6.5 68.5 %all-gather.9.cloned.1.call-start = ((), (), s32[]{:S(2)}) async-start(), calls=%async_computation.3 | async-start | bytes 2048000 | tf_op jit(solution)/shard_map/all_gather | solution.py:71
  6.5 8.5 %copy-start = (bf16[160,160,128]{2,1,0:T(8,128)(2,1)S(1)}, bf16[160,160,128]{2,1,0:T(8,128)(2,1)}, u32[]{:S(2)}) copy-start(bf16[160,160,128]{2,1,0:T(8,128)(2,1)} %param.8) | copy-start | bytes 19660804
  6.5 20.9 %copy-start.3 = (bf16[2,128,512]{2,1,0:T(8,128)(2,1)S(1)}, bf16[2,128,512]{2,1,0:T(8,128)(2,1)}, u32[]{:S(2)}) copy-start(bf16[2,128,512]{2,1,0:T(8,128)(2,1)} %param.11) | copy-start | bytes 786436
  6.5 20.9 %copy-start.5 = (f32[2,128]{1,0:T(2,128)S(1)}, f32[2,128]{1,0:T(2,128)}, u32[]{:S(2)}) copy-start(f32[2,128]{1,0:T(2,128)} %param.10) | copy-start | bytes 3076
  6.5 20.9 %copy-start.6 = (f32[2,128]{1,0:T(2,128)S(1)}, f32[2,128]{1,0:T(2,128)}, u32[]{:S(2)}) copy-start(f32[2,128]{1,0:T(2,128)} %param.9) | copy-start | bytes 3076
  37.0 2.8 copy-start.2
  41.5 83.1 %all-gather.7.cloned.1.call-start = ((), (), s32[]{:S(2)}) async-start(), calls=%async_computation.2 | async-start | bytes 6963200 | tf_op jit(solution)/shard_map/all_gather | solution.py:67
  42.9 136.6 %reduce-scatter.3.cloned.1.call-start = ((), (), s32[]{:S(2)}) async-start(), calls=%async_computation.4 | async-start | bytes 2048000 | tf_op jit(solution)/shard_map/reduce_scatter | solution.py:75
  153.0 8.4 %copy-start.7 = (f32[2,128]{1,0:T(2,128)S(1)}, f32[2,128]{1,0:T(2,128)}, u32[]{:S(2)}) copy-start(f32[2,128]{1,0:T(2,128)} %param.14) | copy-start | bytes 3076
  153.0 8.4 %copy-start.8 = (f32[2,128]{1,0:T(2,128)S(1)}, f32[2,128]{1,0:T(2,128)}, u32[]{:S(2)}) copy-start(f32[2,128]{1,0:T(2,128)} %param.13) | copy-start | bytes 3076
  153.0 8.4 %copy-start.9 = (bf16[2,128,128]{2,1,0:T(8,128)(2,1)S(1)}, bf16[2,128,128]{2,1,0:T(8,128)(2,1)}, u32[]{:S(2)}) copy-start(bf16[2,128,128]{2,1,0:T(8,128)(2,1)} %param.12) | copy-start | bytes 196612
  153.0 29.4 %copy-start.4 = (bf16[2,128,128]{2,1,0:T(8,128)(2,1)S(1)}, bf16[2,128,128]{2,1,0:T(8,128)(2,1)}, u32[]{:S(2)}) copy-start(bf16[2,128,128]{2,1,0:T(8,128)(2,1)} %param.15) | copy-start | bytes 196612
  153.0 63.7 %all-gather.15.cloned.1.call-start = ((), (), s32[]{:S(2)}) async-start(), calls=%async_computation.7 | async-start | bytes 2048000 | tf_op jit(solution)/shard_map/all_gather | solution.py:95
  184.5 4.1 copy-start.1
  186.8 79.4 %all-gather.13.cloned.1.call-start = ((), (), s32[]{:S(2)}) async-start(), calls=%async_computation.6 | async-start | bytes 6963200 | tf_op jit(solution)/shard_map/all_gather | solution.py:88
  188.5 125.4 %all-gather.11.cloned.1.call-start = ((), (), s32[]{:S(2)}) async-start(), calls=%async_computation.5 | async-start | bytes 6963200 | tf_op jit(solution)/shard_map/all_gather | solution.py:87
  189.1 154.0 %reduce-scatter.5.cloned.1.call-start = ((), (), s32[]{:S(2)}) async-start(), calls=%async_computation.8 | async-start | bytes 2048000 | tf_op jit(solution)/shard_map/reduce_scatter | solution.py:99
  294.8 101.5 %all-gather.17.cloned.1.call-start = ((), (), s32[]{:S(2)}) async-start(), calls=%async_computation.9 | async-start | bytes 6963200 | tf_op jit(solution)/shard_map/all_gather | solution.py:107
Sparse Core Ops, SparseCore 0:
  41.6 33.3 all-gather.8
  76.9 47.6 all-gather.6
  153.1 26.3 reduce-scatter.2
  187.0 29.7 all-gather.14
  218.5 47.6 all-gather.12
  268.0 45.8 all-gather.10
  316.6 26.3 reduce-scatter.4
  348.5 47.7 all-gather.16
where the time goes:
time: 411 us; the launch traced here: 410 us
  waiting for transfers between devices  261 us (64%)
  local copies, waits for them, and re-layouts  66.3 us (16%)
  other arithmetic  42 us (10%)
  matrix products  25.9 us (6%)
  between operations  13.8 us (3%)
    all_gather x1, waiting for transfers between devices, on_device(): gathered = lax.all_gather(result, 'depth', axis=0, tiled=True)  47.9 us
    all_gather x1, waiting for transfers between devices, on_device(): lax.all_gather(gated(own_rows, first_w[:, :2 * chans]), 'depth', axis=0,...  45.9 us
    all_gather x1, waiting for transfers between devices, on_device(): lax.all_gather(right_share, 'depth', axis=1, tiled=True)  45.8 us
    all_gather x1, waiting for transfers between devices, on_device(): lax.all_gather(right, 'row', axis=0, tiled=True)  32.1 us
    all_gather x1, waiting for transfers between devices, on_device(): lax.all_gather(left_in, 'col', axis=1, tiled=True)  27.6 us
    reduce_scatter x1, waiting for transfers between devices, on_device(): lax.psum_scatter(partial_in.astype(jnp.bfloat16), 'row', scatter_dimensio...  25.9 us
    all_gather x1, waiting for transfers between devices, on_device(): lax.all_gather(middle, 'depth', axis=1, tiled=True)  18.8 us
    unnamed x22, local copies, waits for them, and re-layouts  17.7 us
  transfers between devices with their start and end apart: 8, of which 8 were waited for; matrix products, arithmetic and copies ran while one was open for 13% of the time, Pallas kernels for 0%

commit v1 on v0

v1 whole, which is shorter than its diff:
```python
import functools

import jax
import jax.numpy as jnp
from jax import lax
from jax.experimental import pallas as pl
from jax.experimental.pallas import tpu as pltpu
from jax.sharding import PartitionSpec as P

F32 = jnp.float32
BF16 = jnp.bfloat16
VMEM_LIMIT = 60 * 1024 * 1024
NT = (((1,), (1,)), ((), ()))


def norm_rows(values, gain, bias):
    mean = jnp.mean(values, axis=-1, keepdims=True)
    centred = values - mean
    spread = jnp.mean(centred * centred, axis=-1, keepdims=True)
    return centred * lax.rsqrt(spread + 1e-05) * gain + bias


def norm_chans(values, gain, bias):
    mean = jnp.mean(values, axis=0, keepdims=True)
    centred = values - mean
    spread = jnp.mean(centred * centred, axis=0, keepdims=True)
    return centred * lax.rsqrt(spread + 1e-05) * gain + bias


def widen_rows(rows):
    return jnp.concatenate([rows, jnp.zeros((256 - rows.shape[0], rows.shape[1]), rows.dtype)], axis=0)


def fold(tail):
    total = tail[:16]
    for m in range(1, 4):
        total = total + pltpu.roll(tail[16 * m : 16 * m + 16], 32 * m, 1)
    return total


def unfold(packed):
    parts = [packed] + [pltpu.roll(packed, 128 - 32 * m, 1) for m in range(1, 4)]
    tail = jnp.concatenate(parts, axis=0)
    lane = lax.broadcasted_iota(jnp.int32, tail.shape, 1)
    return jnp.where(lane < 32, tail, 0.0)


def pack(chans):
    return jnp.concatenate([chans[:, :128], fold(chans[:, 128:])], axis=0).astype(BF16)


def unpack(block):
    wide = block.astype(F32)
    return jnp.concatenate([wide[:64], unfold(wide[64:])], axis=1)


def gated_chans(weight_t, normed):
    hidden = lax.dot_general(weight_t, normed, NT, preferred_element_type=F32)
    n = weight_t.shape[0] // 2
    return jax.nn.sigmoid(hidden[n:]) * hidden[:n]


def share_kernel(x_ref, gain_ref, bias_ref, weight_ref, out_ref):
    rows = x_ref.shape[0]
    for r in range(rows):
        normed = norm_rows(x_ref[r].astype(F32), gain_ref[...], bias_ref[...]).astype(BF16)
        out_ref[r] = pack(gated_chans(weight_ref[...], widen_rows(normed)))


def tile_kernel(steps, per, x_ref, gain_ref, bias_ref, weight_ref, out_ref, main, tail):
    step = pl.program_id(0)
    for r in range(per):
        normed = norm_rows(x_ref[r].astype(F32), gain_ref[...], bias_ref[...]).astype(BF16)
        values = gated_chans(weight_ref[...], widen_rows(normed))
        row = step * per + r
        main[pl.ds(row, 64, stride=160), :] = values[:, :128]
        tail[pl.ds(row, 64, stride=160), :] = values[:, 128:]

    @pl.when(step == steps - 1)
    def _():
        def put(c, carry):
            at = pl.ds(pl.multiple_of(c * 160, 8), 160)
            out_ref[c] = jnp.concatenate([main[at, :], tail[at, :]], axis=1).astype(BF16)
            return carry

        lax.fori_loop(0, 64, put, 0)


def contract_kernel(big_is_packed, *refs):
    if big_is_packed:
        swap_ref, big_ref, small_ref, out_ref, main, tail, bmain, btail = refs
        half = swap_ref[0]

        def spread_big(b, carry):
            z, rest = b // 20, lax.rem(b, 20)
            o, j = rest // 10, lax.rem(rest, 10)
            row = z * 20 + jnp.where(half == 0, o, 1 - o) * 10 + j
            wide = unpack(big_ref[b])
            bmain[pl.ds(row, 64, stride=160), :] = wide[:, :128]
            btail[pl.ds(row, 64, stride=160), :] = wide[:, 128:]
            return carry

        lax.fori_loop(0, 160, spread_big, 0, unroll=4)
    else:
        big_ref, small_ref, out_ref, main, tail = refs

    def spread(b, carry):
        wide = unpack(small_ref[b])
        main[pl.ds(b, 64, stride=80), :] = wide[:, :128]
        tail[pl.ds(b, 64, stride=80), :] = wide[:, 128:]
        return carry

    lax.fori_loop(0, 80, spread, 0, unroll=4)

    def multiply(c, carry):
        at = pl.ds(pl.multiple_of(c * 80, 8), 80)
        small = jnp.concatenate([main[at, :], tail[at, :]], axis=1).astype(BF16)
        if big_is_packed:
            bat = pl.ds(pl.multiple_of(c * 160, 8), 160)
            big = jnp.concatenate([bmain[bat, :], btail[bat, :]], axis=1).astype(BF16)
        else:
            big = big_ref[c]
        product = lax.dot_general(small, big, NT, preferred_element_type=F32)
        main[at, :] = product[:, :128]
        tail[at, :] = jnp.concatenate([product[:, 128:], jnp.zeros((80, 96), F32)], axis=1)
        return carry

    lax.fori_loop(0, 64, multiply, 0, unroll=4)

    def collect(b, carry):
        out_ref[b] = jnp.concatenate(
            [main[pl.ds(b, 64, stride=80), :], fold(tail[pl.ds(b, 64, stride=80), :])], axis=0
        ).astype(BF16)
        return carry

    lax.fori_loop(0, 80, collect, 0, unroll=4)


def middle_kernel(
    own_ref, other_ref, x_ref, gain0_ref, bias0_ref, gatew_ref, ogain_ref, obias_ref, outw_ref,
    gain1_ref, bias1_ref, projw_ref, mid_ref, keep_ref, send_ref,
):
    lane = lax.broadcasted_iota(jnp.int32, (128, 256), 1)
    eye = (lax.broadcasted_iota(jnp.int32, (128, 128), 0) == lax.broadcasted_iota(jnp.int32, (128, 128), 1))
    eye = eye.astype(F32).astype(BF16)
    for s in range(own_ref.shape[0]):
        tri = jnp.concatenate([unpack(own_ref[s]), unpack(other_ref[s])], axis=0)
        upd = norm_chans(tri, ogain_ref[...], obias_ref[...]).astype(BF16)
        turned = jnp.dot(outw_ref[...], upd, preferred_element_type=F32)
        x = x_ref[s]
        normed = norm_rows(x.astype(F32), gain0_ref[...], bias0_ref[...]).astype(BF16)
        gate = jax.nn.sigmoid(
            lax.dot_general(gatew_ref[...], widen_rows(normed), NT, preferred_element_type=F32)
        )
        field = lax.dot_general(eye, widen_rows(x), NT, preferred_element_type=F32)
        middle = (field + gate * turned).astype(BF16)
        wide = middle.astype(F32)
        mid_ref[s] = jnp.transpose(wide)[:160].astype(BF16)
        normed1 = norm_chans(wide, gain1_ref[...], bias1_ref[...]).astype(BF16)
        hidden = jnp.dot(projw_ref[...], normed1, preferred_element_type=F32)
        for side in range(2):
            h = hidden[256 * side : 256 * side + 256]
            value = jnp.where(lane < 160, jax.nn.sigmoid(h[128:]) * h[:128], 0.0)
            keep_ref[side, s] = pack(value[:64])
            send_ref[side, s] = pack(value[64:])


def last_kernel(
    own_ref, other_ref, x_ref, gain_ref, bias_ref, gatew_ref, ogain_ref, obias_ref, outw_ref, out_ref
):
    for s in range(own_ref.shape[0]):
        tri = jnp.concatenate([unpack(own_ref[s]), unpack(other_ref[s])], axis=0)
        upd = norm_chans(tri, ogain_ref[...], obias_ref[...])
        upd = jnp.transpose(upd)[:160].astype(BF16)
        x = x_ref[s].astype(F32)
        normed = norm_rows(x, gain_ref[...], bias_ref[...]).astype(BF16)
        gate = jax.nn.sigmoid(jnp.dot(normed, gatew_ref[...], preferred_element_type=F32))
        turned = jnp.dot(upd, outw_ref[...], preferred_element_type=F32)
        out_ref[s] = (x + gate * turned).astype(BF16)


def params():
    return pltpu.CompilerParams(vmem_limit_bytes=VMEM_LIMIT)


def whole(shape):
    zeros = (0,) * len(shape)
    return pl.BlockSpec(shape, lambda *_: zeros)


def share_call(x, gain, bias, weight_t):
    return pl.pallas_call(
        share_kernel,
        grid=(4,),
        in_specs=[
            pl.BlockSpec((5, 160, 128), lambda b: (b, 0, 0)),
            whole((1, 128)), whole((1, 128)), whole((128, 128)),
        ],
        out_specs=pl.BlockSpec((5, 80, 128), lambda b: (b, 0, 0)),
        out_shape=jax.ShapeDtypeStruct((20, 80, 128), BF16),
        compiler_params=params(),
        name="share",
    )(x, gain, bias, weight_t)


def tile_call(x, gain, bias, weight_t):
    per = 8
    steps = 160 // per
    return pl.pallas_call(
        functools.partial(tile_kernel, steps, per),
        grid=(steps,),
        in_specs=[
            pl.BlockSpec((per, 160, 128), lambda b: (b, 0, 0)),
            whole((1, 128)), whole((1, 128)), whole((128, 128)),
        ],
        out_specs=whole((64, 160, 256)),
        out_shape=jax.ShapeDtypeStruct((64, 160, 256), BF16),
        scratch_shapes=[pltpu.VMEM((64 * 160, 128), F32)] * 2,
        compiler_params=params(),
        cost_estimate=pl.CostEstimate(flops=2 * 25600 * 128 * 128, bytes_accessed=30 * 2**20, transcendentals=25600 * 64),
        name="tile",
    )(x, gain, bias, weight_t)


def contract_call(big, small, half=None):
    packed = half is not None
    scratch = [pltpu.VMEM((64 * 80, 128), F32)] * 2
    args = [big, small]
    specs = [whole(big.shape), whole(small.shape)]
    if packed:
        scratch = scratch + [pltpu.VMEM((64 * 160, 128), F32)] * 2
        args = [half] + args
        specs = [pl.BlockSpec(memory_space=pltpu.SMEM)] + specs
    return pl.pallas_call(
        functools.partial(contract_kernel, packed),
        grid=(1,),
        in_specs=specs,
        out_specs=whole((80, 80, 128)),
        out_shape=jax.ShapeDtypeStruct((80, 80, 128), BF16),
        scratch_shapes=scratch,
        compiler_params=params(),
        name="contract",
    )(*args)


def middle_call(own, other, x, *rest):
    per, steps = 5, 2
    block = pl.BlockSpec((per, 80, 128), lambda b: (b, 0, 0))
    rows = pl.BlockSpec((per, 160, 128), lambda b: (b, 0, 0))
    pair = pl.BlockSpec((2, per, 80, 128), lambda b: (0, b, 0, 0))
    return pl.pallas_call(
        middle_kernel,
        grid=(steps,),
        in_specs=[block, block, rows] + [whole(r.shape) for r in rest],
        out_specs=[rows, pair, pair],
        out_shape=[
            jax.ShapeDtypeStruct((10, 160, 128), BF16),
            jax.ShapeDtypeStruct((2, 10, 80, 128), BF16),
            jax.ShapeDtypeStruct((2, 10, 80, 128), BF16),
        ],
        compiler_params=params(),
        name="middle",
    )(own, other, x, *rest)


def last_call(own, other, x, *rest):
    per, steps = 5, 2
    block = pl.BlockSpec((per, 80, 128), lambda b: (b, 0, 0))
    rows = pl.BlockSpec((per, 160, 128), lambda b: (b, 0, 0))
    return pl.pallas_call(
        last_kernel,
        grid=(steps,),
        in_specs=[block, block, rows] + [whole(r.shape) for r in rest],
        out_specs=rows,
        out_shape=jax.ShapeDtypeStruct((10, 160, 128), BF16),
        compiler_params=params(),
        name="last",
    )(own, other, x, *rest)


def on_device(pair, in_gain, in_bias, proj_weight, gate_weight, out_gain, out_bias, out_weight):
    layer = lax.axis_index("depth")
    z, half = layer // 2, layer % 2
    swap = [(d, d ^ 1) for d in range(16)]
    same_core = [list(range(0, 16, 2)), list(range(1, 16, 2))]

    def local(values, axis):
        return jnp.where(half == 0, values, jnp.roll(values, 64, axis))

    def mine(values):
        return lax.dynamic_slice_in_dim(values, 64 * half, 64, 1)

    p0 = proj_weight[0]
    left_w = jnp.concatenate([mine(p0[:, :128]), mine(p0[:, 128:256])], axis=1).T
    right_w = jnp.concatenate([mine(p0[:, 256:384]), mine(p0[:, 384:])], axis=1).T
    gain0, bias0 = in_gain[0:1], in_bias[0:1]
    share = lax.dynamic_slice_in_dim(pair, 20 * z, 20, 0).reshape(2, 10, 160, 128)
    share = jnp.where(half == 0, share, share[::-1]).reshape(20, 160, 128)
    right = share_call(share, gain0, bias0, right_w)
    right_all = lax.all_gather(right, "row", axis=0, tiled=True)
    left = tile_call(pair, gain0, bias0, left_w)
    products = contract_call(left, right_all)
    sums = lax.psum_scatter(products, "col", scatter_dimension=0, tiled=True)
    other = lax.ppermute(sums[10:], "depth", swap)

    columns = lax.dynamic_slice_in_dim(pair, 10 * layer, 10, 1).transpose(1, 0, 2)
    p1 = proj_weight[1]
    proj1 = jnp.concatenate([local(p1[:, 128 * s : 128 * s + 128], 1) for s in range(4)], axis=1).T
    middle, keep, send = middle_call(
        sums[:10], other, columns, gain0, bias0, gate_weight[0].T,
        local(out_gain[0], 0)[:, None], local(out_bias[0], 0)[:, None], local(out_weight[0], 0).T,
        in_gain[1][:, None], in_bias[1][:, None], proj1,
    )
    got = lax.ppermute(send, "depth", swap)
    left1 = jnp.concatenate([keep[0], got[0]], axis=0)
    right1 = jnp.concatenate([keep[1], got[1]], axis=0)
    right1_all = lax.all_gather(right1, "depth", axis=0, tiled=True, axis_index_groups=same_core)
    left1_all = lax.all_gather(left1, "col", axis=0, tiled=True)
    spread = lax.all_to_all(middle.reshape(10, 16, 10, 128), "depth", 1, 0, tiled=False)
    rows = spread.reshape(160, 10, 128).transpose(1, 0, 2)
    products1 = contract_call(right1_all, left1_all, half.astype(jnp.int32).reshape(1))
    sums1 = lax.psum_scatter(products1, "row", scatter_dimension=0, tiled=True)
    other1 = lax.ppermute(sums1[10:], "depth", swap)
    result = last_call(
        sums1[:10], other1, rows, in_gain[1:2], in_bias[1:2], gate_weight[1],
        local(out_gain[1], 0)[:, None], local(out_bias[1], 0)[:, None], local(out_weight[1], 0),
    )
    return lax.all_gather(result, "depth", axis=0, tiled=True)


def solution(mesh):
    placed = (P("row", "col", None), P(), P(), P(), P(), P(), P(), P())
    return jax.shard_map(
        on_device, mesh=mesh, in_specs=placed, out_specs=P("row", "col", None), check_vma=False
    )
```

time: 411 us -> 304 us (0.74)
  waiting for transfers between devices: 261 us -> 173 us
  Pallas kernels: 0 us -> 76.3 us
  local copies, waits for them, and re-layouts: 66.3 us -> 26.1 us
  other arithmetic: 42 us -> 6.2 us
  matrix products: 25.9 us -> 0 us
  starting transfers between devices: 0.69 us -> 7.47 us
    all_gather x6 -> x4, waiting for transfers between devices: 218 us -> 132 us  [the longest x1 48 us: on_device(): lax.all_gather(right1, 'depth', axis=0, tiled=True, axis_index_groups=sam...]
    pallas_call x0 -> x6, Pallas kernels: none -> 76.3 us  [the longest x2 37.1 us: contract_call(): pl.pallas_call(functools.partial(contract_kernel, packed), grid=(1,), in_...]
    all_gather x4 -> x0, local copies, waits for them, and re-layouts: 37.4 us -> none  [the longest x1 15.1 us: on_device(): lax.all_gather(gated(own_rows, first_w[:, :2 * chans]), 'depth', axis=0,...]
    reduce_sum x9 -> x0, other arithmetic: 28.4 us -> none  [the longest x5 17 us: normalize(): spread = jnp.mean(centred * centred, axis=-1, keepdims=True)]
    dot_general x10 -> x0, matrix products: 25.9 us -> none  [the longest x1 8.86 us: on_device(): jnp.einsum('kic,kjc->ijc', lax.all_gather(left_in, 'col', axis=1, tiled=T...]
    convert_element_type x5 -> x0, other arithmetic: 13.5 us -> none  [the longest x1 9.51 us: on_device(): normed = normalize(pair, in_gain[0], in_bias[0]).astype(jnp.bfloat16)]
    convert_element_type x2 -> x0, local copies, waits for them, and re-layouts: 9.27 us -> none  [the longest x1 4.66 us: on_device(): partial_in.astype(jnp.bfloat16)]
    unnamed x22 -> x18, local copies, waits for them, and re-layouts: 17.7 us -> 9.84 us
  transfers between devices with their start and end apart: 8 -> 10, of which waited for: 8 -> 8; matrix products, arithmetic and copies ran while one was open for 13% -> 5% of each run, Pallas kernels for 0% -> 8%
where the time goes in v1:
time: 304 us; the launch traced here: 303 us
  waiting for transfers between devices  173 us (57%)
  Pallas kernels  76.3 us (25%)
  local copies, waits for them, and re-layouts  26.1 us (9%)
  between operations  13.6 us (4%)
  starting transfers between devices  7.47 us (2%)
  other arithmetic  6.2 us (2%)
    all_gather x1, waiting for transfers between devices, on_device(): lax.all_gather(right1, 'depth', axis=0, tiled=True, axis_index_groups=sam...  48 us
    all_gather x1, waiting for transfers between devices, on_device(): return lax.all_gather(result, 'depth', axis=0, tiled=True)  47.1 us
    pallas_call x2, Pallas kernels, contract_call(): pl.pallas_call(functools.partial(contract_kernel, packed), grid=(1,), in_...  37.1 us
    all_gather x1, waiting for transfers between devices, on_device(): left1_all = lax.all_gather(left1, 'col', axis=0, tiled=True)  28.3 us
    pallas_call x1, Pallas kernels, tile_call(): pl.pallas_call(functools.partial(tile_kernel, steps, per), grid=(steps,),...  24.4 us
    reduce_scatter x1, waiting for transfers between devices, on_device(): sums1 = lax.psum_scatter(products1, 'row', scatter_dimension=0, tiled=True)  20.2 us
    reduce_scatter x1, waiting for transfers between devices, on_device(): sums = lax.psum_scatter(products, 'col', scatter_dimension=0, tiled=True)  20 us
    unnamed x18, local copies, waits for them, and re-layouts  9.84 us
  transfers between devices with their start and end apart: 10, of which 8 were waited for; matrix products, arithmetic and copies ran while one was open for 5% of the time, Pallas kernels for 8%

profile of v1, /device:TPU:1, one launch (start us, length us, event | category | flops | bytes accessed | tf_op | source)
XLA Modules:
  0.0 302.9 jit_solution(13743802849138720530)
XLA Ops:
  6.5 1.0 slice_bitcast_fusion.4
  7.7 1.4 fusion.5
  9.7 1.2 constant_dynamic-slice_fusion.3
  10.9 1.1 reverse_select_fusion
  11.9 4.4 %share.1 = bf16[20,80,128]{2,1,0:T(8,128)(2,1)} custom-call(bf16[20,160,128]{2,1,0:T(8,128)(2,1)} %bitcast.79, f32[1,128]{1,0:T(1,128)} %get-tuple-element.67.gain_ref.gain0_ref, f32[1,128]{1,0:T(1,128)} %get-tuple-element.59.bias_ref.bias0_ref, bf16[128,128]{1,0:T(8,128)(2,1)} %maximum_bitcast_fusion.2.weight_ref), custom_call_target="tpu_custom_call" | custom-call | tf_op jit(solution)/shard_map/share/pallas_call | solution.py:192
  17.0 24.4 %tile.1.refs_0_ = bf16[64,160,256]{2,1,0:T(8,128)(2,1)} custom-call(bf16[160,160,128]{2,1,0:T(8,128)(2,1)} %x_ref.1, f32[1,128]{1,0:T(1,128)} %get-tuple-element.67.gain_ref.gain0_ref, f32[1,128]{1,0:T(1,128)} %get-tuple-element.59.bias_ref.bias0_ref, bf16[128,128]{1,0:T(8,128)(2,1)} %maximum_bitcast_fusion.1.weight_ref), custom_call_target="tpu_custom_call" | custom-call | flops 838860800 | bytes 31457280 | tf_op jit(solution)/shard_map/tile/pallas_call | solution.py:209
  41.4 8.5 %all-gather.5.cloned.1.call-done.refs_1_ = bf16[80,80,128]{2,1,0:T(8,128)(2,1)} async-done(((bf16[20,80,128]{2,1,0:T(8,128)(2,1)}), bf16[80,80,128]{2,1,0:T(8,128)(2,1)}) %all-gather.5.cloned.1.call-update) | async-done | bytes 1638416 | tf_op jit(solution)/shard_map/all_gather | solution.py:300
  49.9 12.9 %contract.2 = bf16[80,80,128]{2,1,0:T(8,128)(2,1)} custom-call(bf16[64,160,256]{2,1,0:T(8,128)(2,1)} %tile.1.refs_0_, bf16[80,80,128]{2,1,0:T(8,128)(2,1)} %all-gather.5.cloned.1.call-done.refs_1_), custom_call_target="tpu_custom_call" | custom-call | tf_op jit(solution)/shard_map/contract/pallas_call | solution.py:234
  63.4 0.7 copy.58.bias1_ref
  64.1 0.7 copy.57.gain1_ref
  67.3 0.8 copy.59.projw_ref
  68.7 1.5 constant_dynamic-slice_fusion
  70.3 0.9 copy.72
  71.1 20.0 %reduce-scatter.3.cloned.1.call-done = bf16[20,80,128]{2,1,0:T(8,128)(2,1)} async-done(((bf16[80,80,128]{2,1,0:T(8,128)(2,1)}), bf16[20,80,128]{2,1,0:T(8,128)(2,1)}) %reduce-scatter.3.cloned.1.call-update) | async-done | bytes 409616 | tf_op jit(solution)/shard_map/reduce_scatter | solution.py:303
  91.1 1.7 fusion.2
  92.9 1.0 collective-permute-start
  95.6 6.2 %middle.1 = (bf16[10,160,128]{2,1,0:T(8,128)(2,1)}, bf16[2,10,80,128]{3,2,1,0:T(8,128)(2,1)}, bf16[2,10,80,128]{3,2,1,0:T(8,128)(2,1)}) custom-call(bf16[10,80,128]{2,1,0:T(8,128)(2,1)} %get-tuple-element.18.own_ref, bf16[10,80,128]{2,1,0:T(8,128)(2,1)} %copy-done.3, bf16[10,160,128]{2,1,0:T(8,128)(2,1)} %bitcast.81, ...), custom_call_target="tpu_custom_call" | custom-call | tf_op jit(solution)/shard_map/middle/pallas_call | solution.py:251
  102.2 1.1 slice_bitcast_fusion.2
  103.8 0.8 pad_maximum_fusion.1
  104.7 0.8 pad_maximum_fusion
  105.5 28.3 %all-gather.9.cloned.1.call-done.refs_2_ = bf16[80,80,128]{2,1,0:T(8,128)(2,1)} async-done(((bf16[20,80,128]{2,1,0:T(8,128)(2,1)}), bf16[80,80,128]{2,1,0:T(8,128)(2,1)}) %all-gather.9.cloned.1.call-update) | async-done | bytes 1638416 | tf_op jit(solution)/shard_map/all_gather | solution.py:318
  133.9 48.0 %all-gather.7.cloned.1.call-done.refs_1_ = bf16[160,80,128]{2,1,0:T(8,128)(2,1)} async-done(((bf16[20,80,128]{2,1,0:T(8,128)(2,1)}), bf16[160,80,128]{2,1,0:T(8,128)(2,1)}) %all-gather.7.cloned.1.call-update) | async-done | bytes 3276816 | tf_op jit(solution)/shard_map/all_gather | solution.py:317
  181.8 24.2 %contract.3 = bf16[80,80,128]{2,1,0:T(8,128)(2,1)} custom-call(s32[1]{0:T(128)} %bitcast.refs_0_, bf16[160,80,128]{2,1,0:T(8,128)(2,1)} %all-gather.7.cloned.1.call-done.refs_1_, bf16[80,80,128]{2,1,0:T(8,128)(2,1)} %all-gather.9.cloned.1.call-done.refs_2_), custom_call_target="tpu_custom_call" | custom-call | tf_op jit(solution)/shard_map/contract/pallas_call | solution.py:234
  206.2 0.9 copy.60
  207.2 5.0 %all-to-all-start = ((bf16[1,10,16,10,128]{4,3,1,0,2:T(8,128)(2,1)}), bf16[1,10,16,10,128]{4,3,1,0,2:T(8,128)(2,1)S(1)}, u32[]{:S(2)}, u32[]{:S(2)}) async-start(bf16[1,10,16,10,128]{4,3,1,0,2:T(8,128)(2,1)} %copy.60), calls=%async_computation.2 | async-start | bytes 1310720 | tf_op jit(solution)/shard_map/all_to_all | solution.py:319
  212.8 20.2 %reduce-scatter.5.cloned.1.call-done = bf16[20,80,128]{2,1,0:T(8,128)(2,1)} async-done(((bf16[80,80,128]{2,1,0:T(8,128)(2,1)}), bf16[20,80,128]{2,1,0:T(8,128)(2,1)}) %reduce-scatter.5.cloned.1.call-update) | async-done | bytes 409616 | tf_op jit(solution)/shard_map/reduce_scatter | solution.py:322
  233.1 1.7 fusion.1
  234.8 0.9 collective-permute-start.2
  236.4 0.9 copy.73
  237.9 4.3 %last.1 = bf16[10,160,128]{2,1,0:T(8,128)(2,1)} custom-call(bf16[10,80,128]{2,1,0:T(8,128)(2,1)} %get-tuple-element.12.own_ref, bf16[10,80,128]{2,1,0:T(8,128)(2,1)} %copy-done.2, bf16[10,160,128]{2,1,0:T(8,128)(2,1)} %bitcast.82, f32[1,128]{1,0:T(1,128)} %get-tuple-element.69.gain_ref, f32[1,128]{1,0:T(1,128)} %get-tuple-element.57.bias_ref, ...), custom_call_target="tpu_custom_call" | custom-call | tf_op jit(solution)/shard_map/last/pallas_call | solution.py:270
  242.2 47.1 %all-gather.11.cloned.1.call-done = bf16[160,160,128]{2,1,0:T(8,128)(2,1)} async-done(((bf16[10,160,128]{2,1,0:T(8,128)(2,1)}), bf16[160,160,128]{2,1,0:T(8,128)(2,1)}) %all-gather.11.cloned.1.call-update) | async-done | bytes 6553616 | tf_op jit(solution)/shard_map/all_gather | solution.py:328
  289.3 6.8 %copy.75 = bf16[160,160,128]{2,1,0:T(8,128)(2,1)} copy(bf16[160,160,128]{2,1,0:T(8,128)(2,1)} %all-gather.11.cloned.1.call-done) | data formatting | bytes 13107200
  (64 shorter events, 10.1 us)
Async XLA Ops:
  6.5 43.4 %all-gather.5.cloned.1.call-start = ((), (), s32[]{:S(2)}) async-start(), calls=%async_computation.3 | async-start | bytes 2048000 | tf_op jit(solution)/shard_map/all_gather | solution.py:300
  16.4 74.8 %reduce-scatter.3.cloned.1.call-start = ((), (), s32[]{:S(2)}) async-start(), calls=%async_computation.4 | async-start | bytes 2048000 | tf_op jit(solution)/shard_map/reduce_scatter | solution.py:303
  41.4 21.5 %copy-start.5 = (f32[2,128]{1,0:T(2,128)S(1)}, f32[2,128]{1,0:T(2,128)}, u32[]{:S(2)}) copy-start(f32[2,128]{1,0:T(2,128)} %param.14) | copy-start | bytes 3076
  41.4 21.7 %copy-start.6 = (f32[2,128]{1,0:T(2,128)S(1)}, f32[2,128]{1,0:T(2,128)}, u32[]{:S(2)}) copy-start(f32[2,128]{1,0:T(2,128)} %param.13) | copy-start | bytes 3076
  41.4 23.7 %copy-start.4 = (bf16[2,128,128]{2,1,0:T(8,128)(2,1)S(1)}, bf16[2,128,128]{2,1,0:T(8,128)(2,1)}, u32[]{:S(2)}) copy-start(bf16[2,128,128]{2,1,0:T(8,128)(2,1)} %param.12) | copy-start | bytes 196612
  41.4 25.0 %copy-start.1 = (bf16[2,128,128]{2,1,0:T(8,128)(2,1)S(1)}, bf16[2,128,128]{2,1,0:T(8,128)(2,1)}, u32[]{:S(2)}) copy-start(bf16[2,128,128]{2,1,0:T(8,128)(2,1)} %param.15) | copy-start | bytes 196612
  62.8 71.1 %all-gather.9.cloned.1.call-start = ((), (), s32[]{:S(2)}) async-start(), calls=%async_computation.6 | async-start | bytes 2048000 | tf_op jit(solution)/shard_map/all_gather | solution.py:318
  92.9 2.1 collective-permute-start
  94.9 0.7 copy-start.3
  101.8 2.0 collective-permute-start.1
  103.8 102.3 %copy-start = (bf16[10,160,128]{2,1,0:T(8,128)(2,1)S(1)}, bf16[10,160,128]{2,1,0:T(8,128)(2,1)}, u32[]{:S(2)}) copy-start(bf16[10,160,128]{2,1,0:T(8,128)(2,1)} %get-tuple-element.10) | copy-start | bytes 1228804
  104.6 77.2 %all-gather.7.cloned.1.call-start = ((), (), s32[]{:S(2)}) async-start(), calls=%async_computation.5 | async-start | bytes 3686400 | tf_op jit(solution)/shard_map/all_gather | solution.py:317
  105.5 127.6 %reduce-scatter.5.cloned.1.call-start = ((), (), s32[]{:S(2)}) async-start(), calls=%async_computation.7 | async-start | bytes 2048000 | tf_op jit(solution)/shard_map/reduce_scatter | solution.py:322
  207.2 29.2 %all-to-all-start = ((bf16[1,10,16,10,128]{4,3,1,0,2:T(8,128)(2,1)}), bf16[1,10,16,10,128]{4,3,1,0,2:T(8,128)(2,1)S(1)}, u32[]{:S(2)}, u32[]{:S(2)}) async-start(bf16[1,10,16,10,128]{4,3,1,0,2:T(8,128)(2,1)} %copy.60), calls=%async_computation.2 | async-start | bytes 1310720 | tf_op jit(solution)/shard_map/all_to_all | solution.py:319
  212.2 77.1 %all-gather.11.cloned.1.call-start = ((), (), s32[]{:S(2)}) async-start(), calls=%async_computation.8 | async-start | bytes 6963200 | tf_op jit(solution)/shard_map/all_gather | solution.py:328
  234.8 2.4 collective-permute-start.2
  237.3 0.7 copy-start.2
Sparse Core Ops, SparseCore 0:
  16.5 33.3 all-gather.4
  62.9 28.1 reduce-scatter.2
  104.7 29.0 all-gather.8
  135.6 46.1 all-gather.6
  206.2 26.8 reduce-scatter.4
  242.3 46.9 all-gather.10
